TPU v7x, 512 devices: a whole 4x8x8 slice. The times are simulated.
512 devices in a mesh: ctx: 32 (over z, y_lo), grp: 16 (over y_hi, x, core).
Axes of the slice: x: 4, y: 8 (y_hi: 2, y_lo: 4; y = y_hi * 4 + y_lo), z: 8, core: 2. Of those that a mesh axis runs over, the one named last changes fastest.
Arguments:
- queries: bfloat16 [16384, 8192], P('ctx', 'grp'), may hold values from -48 to 48
- kv_cols: bfloat16 [16384, 2048], P('ctx', 'grp'), may hold values from -8 to 8
- lengths: int32 [16], replicated, may hold values from 1 to 2048, 16384 in all
- page_owner: int32 [1024, 1], P('ctx'), may hold values from 0 to 31; in each aligned block of 32 rows (0 to 31, 32 to 63, ...) at most 2 rows name the same one
Outputs:
- attended: bfloat16 [16384, 8192], P('ctx', 'grp')
- decode_cache: bfloat16 [2048, 16, 2048], P('ctx', None, 'grp')
Inputs may be any that keep to these rules, and one draw needn't show every extreme that they name: The lengths sum to 16384; the longest request has exactly 2048 tokens. `page_owner`: among the 32 pages of one device no owner is named more than 2 times, a bound that some block reaches.
All inputs are finite; a program needn't handle non-finite values.
Results may differ from a plain program's by a relative error of at most 0.004.
Values may be sent and summed in bfloat16 or wider, within the bound.
A program may use at most 64 MiB of HBM per device.

v0:
```python
import jax
import jax.numpy as jnp
from jax import lax
from jax.sharding import PartitionSpec as P

SPAN = 4
PAGE = 16
CAP = 2


def swapped(value, axis, distance):
    mask = 2**distance
    pairs = [(source, source ^ mask) for source in range(lax.axis_size(axis))]
    return lax.ppermute(value, axis, pairs)


def passed_along(value, axis, steps):
    count = lax.axis_size(axis)
    leading, last = (max(0, -steps), min(count, count - steps))
    return lax.ppermute(value, axis, [(source, source + steps) for source in range(leading, last)])


def segment_of(positions, doc_ends):
    return jnp.sum((doc_ends[None, :] <= positions[:, None]).astype(jnp.int32), axis=1)


def hand_over(kv_cols, page_owner, ctx_count):
    page_count = page_owner.shape[0]
    head_dim = kv_cols.shape[1]
    owners = page_owner[:, 0]
    onehot = (owners[:, None] == jnp.arange(ctx_count, dtype=jnp.int32)[None, :]).astype(jnp.int32)
    earlier = jnp.cumsum(onehot, axis=0) - onehot
    slot_rank = jnp.sum(earlier * onehot, axis=1)
    target = owners * CAP + slot_rank
    selector = (target[None, :] == jnp.arange(ctx_count * CAP, dtype=jnp.int32)[:, None]).astype(
        jnp.bfloat16
    )
    page_rows = kv_cols.reshape(page_count, PAGE * head_dim)
    outgoing = jnp.dot(selector, page_rows, preferred_element_type=jnp.float32).astype(jnp.bfloat16)
    outgoing = outgoing.reshape(ctx_count * CAP, PAGE, head_dim)
    return lax.all_to_all(outgoing, "ctx", split_axis=0, concat_axis=0, tiled=True)


def per_device(queries, kv_cols, lengths, page_owner):
    tok_rows = queries.shape[0]
    head_dim = kv_cols.shape[1]
    head_count = queries.shape[1] // head_dim
    ctx_count = lax.axis_size("ctx")
    partner = swapped(kv_cols, "grp", 0)
    is_even = lax.axis_index("grp") % 2 == 0
    key_rows = jnp.where(is_even, kv_cols, partner)
    value_rows = jnp.where(is_even, partner, kv_cols)
    own_pair = jnp.stack([key_rows, value_rows])
    doc_ends = jnp.cumsum(lengths)
    query_start = lax.axis_index("ctx") * tok_rows
    query_pos = query_start + jnp.arange(tok_rows, dtype=jnp.int32)
    query_seg = segment_of(query_pos, doc_ends)
    score_scale = head_dim ** (-0.5)
    head_queries = [
        queries[:, head_index * head_dim : (head_index + 1) * head_dim]
        for head_index in range(head_count)
    ]

    def attend(carried, kv_block, allowed):
        maxima, totals, accumulators = carried
        new_maxima, new_totals, new_accums = ([], [], [])
        for head_index in range(head_count):
            scores = (
                lax.dot_general(
                    head_queries[head_index],
                    kv_block[0],
                    (((1,), (1,)), ((), ())),
                    preferred_element_type=jnp.float32,
                )
                * score_scale
            )
            scores = jnp.where(allowed, scores, -jnp.inf)
            running = jnp.maximum(maxima[head_index], jnp.max(scores, axis=1))
            correction = jnp.exp(maxima[head_index] - running)
            weights = jnp.exp(scores - running[:, None])
            new_totals.append(totals[head_index] * correction + jnp.sum(weights, axis=1))
            product = jnp.dot(
                weights.astype(jnp.bfloat16), kv_block[1], preferred_element_type=jnp.float32
            )
            new_accums.append(accumulators[head_index] * correction[:, None] + product)
            new_maxima.append(running)
        return (new_maxima, new_totals, new_accums)

    def visit(carried, kv_block, distance):
        key_pos = query_start - distance * tok_rows + jnp.arange(tok_rows, dtype=jnp.int32)
        same_doc = segment_of(key_pos, doc_ends)[None, :] == query_seg[:, None]
        allowed = (key_pos[None, :] <= query_pos[:, None]) & (key_pos[None, :] >= 0) & same_doc
        return attend(carried, kv_block, allowed)

    initial = (
        [jnp.full((tok_rows,), -jnp.inf, jnp.float32) for head_index in range(head_count)],
        [jnp.zeros((tok_rows,), jnp.float32) for head_index in range(head_count)],
        [jnp.zeros((tok_rows, head_dim), jnp.float32) for head_index in range(head_count)],
    )
    carried = visit(initial, own_pair, 0)
    moving = own_pair
    for distance in range(1, SPAN + 1):
        moving = passed_along(moving, "ctx", 1)
        carried = visit(carried, moving, distance)
    maxima, totals, accumulators = carried
    attended = jnp.concatenate(
        [
            accumulators[head_index] / totals[head_index][:, None]
            for head_index in range(head_count)
        ],
        axis=1,
    ).astype(jnp.bfloat16)
    decode_cache = hand_over(kv_cols, page_owner, ctx_count)
    return (attended, decode_cache)


def solution(mesh):
    in_specs = (P("ctx", "grp"), P("ctx", "grp"), P(), P("ctx", None))
    out_specs = (P("ctx", "grp"), P("ctx", None, "grp"))
    return jax.shard_map(
        per_device, mesh=mesh, in_specs=in_specs, out_specs=out_specs, check_vma=False
    )
```

profile of v0, /device:TPU:258, one launch (start us, length us, event | category | flops | bytes accessed | tf_op | source)
XLA Modules:
  0.0 101.4 jit_solution(3686411419564315339)
XLA Ops:
  0.6 1.9 %collective-permute-start = (bf16[512,128]{1,0:T(8,128)(2,1)}, bf16[512,128]{1,0:T(8,128)(2,1)S(1)}, u32[]{:S(2)}, u32[]{:S(2)}) collective-permute-start(bf16[512,128]{1,0:T(8,128)(2,1)} %param.5), channel_id=1, source_target_pairs={{0,1},{1,0},{2,3},{3,2},{4,5},{5,4},{6,7},{7,6},{8,9},{9,8},{10,11... | collective-permute-start | bytes 393224 | tf_op jit(solution)/shard_map/ppermute | solution.py:14
  2.6 1.0 reshape.522
  3.5 0.6 copy-done.25
  4.7 0.7 copy.12
  5.5 10.6 %all-to-all-start = ((bf16[64,16,128]{2,1,0:T(8,128)(2,1)}), bf16[64,16,128]{2,1,0:T(8,128)(2,1)S(1)}, u32[]{:S(2)}, u32[]{:S(2)}) async-start(bf16[64,16,128]{2,1,0:T(8,128)(2,1)} %bitcast.33), calls=%async_computation | async-start | bytes 524288 | tf_op jit(solution)/shard_map/all_to_all | solution.py:41
  16.7 0.5 broadcast_compare_fusion.1
  17.2 0.6 broadcast_compare_fusion.2
  17.8 0.7 copy-done.31
  18.8 0.7 convert_reduce_fusion
  21.5 3.4 %collective-permute-start.1 = (bf16[2,512,128]{2,1,0:T(8,128)(2,1)S(1)}, bf16[2,512,128]{2,1,0:T(8,128)(2,1)}, u32[]{:S(2)}, u32[]{:S(2)}) collective-permute-start(bf16[2,512,128]{2,1,0:T(8,128)(2,1)S(1)} %pad_maximum_fusion.1), channel_id=1, source_target_pairs={{0,16},{16,32},{32,48},{48,64},{64,80},{80,96},{96,112},{112,128},... | collective-permute-start | bytes 786440 | tf_op jit(solution)/shard_map/ppermute | solution.py:20
  24.9 0.8 fusion.99
  25.7 0.8 fusion.89
  26.5 0.8 fusion.79
  27.2 0.8 fusion.69
  28.0 7.5 %collective-permute-done.1 = bf16[2,512,128]{2,1,0:T(8,128)(2,1)} collective-permute-done((bf16[2,512,128]{2,1,0:T(8,128)(2,1)S(1)}, bf16[2,512,128]{2,1,0:T(8,128)(2,1)}, u32[]{:S(2)}, u32[]{:S(2)}) %collective-permute-start.1) | collective-permute-done | bytes 262176 | tf_op jit(solution)/shard_map/ppermute | solution.py:20
  35.6 1.9 %collective-permute-start.2 = (bf16[2,512,128]{2,1,0:T(8,128)(2,1)}, bf16[2,512,128]{2,1,0:T(8,128)(2,1)}, u32[]{:S(2)}, u32[]{:S(2)}) collective-permute-start(bf16[2,512,128]{2,1,0:T(8,128)(2,1)} %collective-permute-done.1), channel_id=1, source_target_pairs={{0,16},{16,32},{32,48},{48,64},{64,80},{80,96},{96,112},{112,128},... | collective-permute-start | bytes 786440 | tf_op jit(solution)/shard_map/ppermute | solution.py:20
  37.5 2.9 %fusion.183 = (f32[512]{0:T(512)}, f32[512,512]{0,1:T(8,128)}) fusion(bf16[512,512]{1,0:T(8,128)(2,1)S(1)} %copy-done.32, bf16[2,512,128]{2,1,0:T(8,128)(2,1)} %collective-permute-done.1, s32[512]{0:T(512)S(1)} %get-tuple-element.12, s32[512]{0:T(512)S(1)} %get-tuple-element.9, pred[512]{0:T(512)(128)(4,1)S(1)} %broadcast_compare_fusion.3, ...), kind=kOutput, calls=%fused_computation.280 | convolution fusion | flops 68943360 | bytes 1321472 | tf_op jit(solution)/shard_map/dot_general | solution.py:69
  40.4 2.9 %fusion.188 = (f32[512]{0:T(512)}, f32[512,512]{0,1:T(8,128)}) fusion(bf16[512,512]{1,0:T(8,128)(2,1)S(1)} %copy-done.32, bf16[2,512,128]{2,1,0:T(8,128)(2,1)} %collective-permute-done.1, s32[512]{0:T(512)S(1)} %get-tuple-element.12, s32[512]{0:T(512)S(1)} %get-tuple-element.9, pred[512]{0:T(512)(128)(4,1)S(1)} %broadcast_compare_fusion.3, ...), kind=kOutput, calls=%fused_computation.285 | convolution fusion | flops 68943360 | bytes 1321472 | tf_op jit(solution)/shard_map/dot_general | solution.py:69
  43.4 2.9 %fusion.193 = (f32[512]{0:T(512)}, f32[512,512]{0,1:T(8,128)}) fusion(bf16[512,512]{1,0:T(8,128)(2,1)S(1)} %copy-done.32, bf16[2,512,128]{2,1,0:T(8,128)(2,1)} %collective-permute-done.1, s32[512]{0:T(512)S(1)} %get-tuple-element.12, s32[512]{0:T(512)S(1)} %get-tuple-element.9, pred[512]{0:T(512)(128)(4,1)S(1)} %broadcast_compare_fusion.3, ...), kind=kOutput, calls=%fused_computation.290 | convolution fusion | flops 68943360 | bytes 1321472 | tf_op jit(solution)/shard_map/dot_general | solution.py:69
  46.3 2.0 %fusion.198 = (f32[512]{0:T(512)}, f32[512,512]{0,1:T(8,128)S(1)}) fusion(bf16[512,512]{1,0:T(8,128)(2,1)} %param.4, bf16[2,512,128]{2,1,0:T(8,128)(2,1)} %collective-permute-done.1, s32[512]{0:T(512)S(1)} %get-tuple-element.12, s32[512]{0:T(512)S(1)} %get-tuple-element.9, pred[512]{0:T(512)(128)(4,1)} %copy-done.37, s32[512]{0:T(512)} %copy-done.12, ...), kind=kOutput, calls=%fused_computation.295 | convolution fusion | flops 68943360 | bytes 1321472 | tf_op jit(solution)/shard_map/dot_general | solution.py:69
  48.3 0.7 collective-permute-done.2
  49.0 1.9 %collective-permute-start.3 = (bf16[2,512,128]{2,1,0:T(8,128)(2,1)}, bf16[2,512,128]{2,1,0:T(8,128)(2,1)S(1)}, u32[]{:S(2)}, u32[]{:S(2)}) collective-permute-start(bf16[2,512,128]{2,1,0:T(8,128)(2,1)} %collective-permute-done.2), channel_id=1, source_target_pairs={{0,16},{16,32},{32,48},{48,64},{64,80},{80,96},{96,112},{112,128},... | collective-permute-start | bytes 786440 | tf_op jit(solution)/shard_map/ppermute | solution.py:20
  50.9 1.5 %fusion.181 = (f32[512]{0:T(512)S(1)}, f32[512,512]{0,1:T(8,128)S(1)}) fusion(bf16[512,512]{1,0:T(8,128)(2,1)} %param.4, bf16[2,512,128]{2,1,0:T(8,128)(2,1)} %collective-permute-done.2, s32[512]{0:T(512)} %copy-done.27, s32[512]{0:T(512)} %get-tuple-element.10, pred[512]{0:T(512)(128)(4,1)S(1)} %copy-done.36, s32[512]{0:T(512)} %copy-done.12, ...), kind=kOutput, calls=%fused_computation.278 | convolution fusion | flops 68943360 | bytes 1321472 | tf_op jit(solution)/shard_map/dot_general | solution.py:69
  52.5 1.4 %fusion.186 = (f32[512]{0:T(512)S(1)}, f32[512,512]{0,1:T(8,128)S(1)}) fusion(bf16[512,512]{1,0:T(8,128)(2,1)S(1)} %copy-done.33, bf16[2,512,128]{2,1,0:T(8,128)(2,1)} %collective-permute-done.2, s32[512]{0:T(512)S(1)} %copy-done.28, s32[512]{0:T(512)S(1)} %copy-done.30, pred[512]{0:T(512)(128)(4,1)S(1)} %copy-done.36, s32[512]{0:T(512)S(1)} %copy-done.13, ...), kind=kOutput, calls=%fused_computation.283 | convolution fusion | flops 68943360 | bytes 1321472 | tf_op jit(solution)/shard_map/dot_general | solution.py:69
  53.9 1.4 %fusion.191 = (f32[512]{0:T(512)S(1)}, f32[512,512]{0,1:T(8,128)S(1)}) fusion(bf16[512,512]{1,0:T(8,128)(2,1)S(1)} %copy-done.33, bf16[2,512,128]{2,1,0:T(8,128)(2,1)} %collective-permute-done.2, s32[512]{0:T(512)S(1)} %copy-done.28, s32[512]{0:T(512)S(1)} %copy-done.30, pred[512]{0:T(512)(128)(4,1)S(1)} %copy-done.36, s32[512]{0:T(512)S(1)} %copy-done.13, ...), kind=kOutput, calls=%fused_computation.288 | convolution fusion | flops 68943360 | bytes 1321472 | tf_op jit(solution)/shard_map/dot_general | solution.py:69
  55.3 1.4 %fusion.196 = (f32[512]{0:T(512)S(1)}, f32[512,512]{0,1:T(8,128)S(1)}) fusion(bf16[512,512]{1,0:T(8,128)(2,1)S(1)} %copy-done.33, bf16[2,512,128]{2,1,0:T(8,128)(2,1)} %collective-permute-done.2, s32[512]{0:T(512)S(1)} %copy-done.28, s32[512]{0:T(512)S(1)} %copy-done.30, pred[512]{0:T(512)(128)(4,1)S(1)} %copy-done.36, s32[512]{0:T(512)S(1)} %copy-done.13, ...), kind=kOutput, calls=%fused_computation.293 | convolution fusion | flops 68943360 | bytes 1321472 | tf_op jit(solution)/shard_map/dot_general | solution.py:69
  56.7 4.9 %collective-permute-done.3 = bf16[2,512,128]{2,1,0:T(8,128)(2,1)S(1)} collective-permute-done((bf16[2,512,128]{2,1,0:T(8,128)(2,1)}, bf16[2,512,128]{2,1,0:T(8,128)(2,1)S(1)}, u32[]{:S(2)}, u32[]{:S(2)}) %collective-permute-start.3) | collective-permute-done | bytes 262176 | tf_op jit(solution)/shard_map/ppermute | solution.py:20
  61.6 2.1 %collective-permute-start.4 = (bf16[2,512,128]{2,1,0:T(8,128)(2,1)S(1)}, bf16[2,512,128]{2,1,0:T(8,128)(2,1)S(1)}, u32[]{:S(2)}, u32[]{:S(2)}) collective-permute-start(bf16[2,512,128]{2,1,0:T(8,128)(2,1)S(1)} %collective-permute-done.3), channel_id=1, source_target_pairs={{0,16},{16,32},{32,48},{48,64},{64,80},{80,96},{96,112},{112,128},... | collective-permute-start | bytes 786440 | tf_op jit(solution)/shard_map/ppermute | solution.py:20
  65.7 8.1 %collective-permute-done.4 = bf16[2,512,128]{2,1,0:T(8,128)(2,1)S(1)} collective-permute-done((bf16[2,512,128]{2,1,0:T(8,128)(2,1)S(1)}, bf16[2,512,128]{2,1,0:T(8,128)(2,1)S(1)}, u32[]{:S(2)}, u32[]{:S(2)}) %collective-permute-start.4) | collective-permute-done | bytes 262176 | tf_op jit(solution)/shard_map/ppermute | solution.py:20
  74.3 0.7 copy-done.24
  75.2 0.9 copy-done.6
  76.9 1.2 %fusion.112 = f32[512,128]{0,1:T(8,128)S(1)} fusion(f32[512,512]{0,1:T(8,128)S(1)} %copy-done.6, f32[512]{0:T(512)S(1)} %get-tuple-element.48, bf16[2,512,128]{2,1,0:T(8,128)(2,1)} %collective-permute-done.1), kind=kOutput, calls=%fused_computation.171 | convolution fusion | flops 67633152 | bytes 1443840 | tf_op jit(solution)/shard_map/dot_general | solution.py:82
  78.9 0.7 copy-done.23
  79.9 0.9 copy-done.3
  81.5 1.2 %fusion.118 = f32[512,128]{0,1:T(8,128)S(1)} fusion(f32[512,512]{0,1:T(8,128)S(1)} %copy-done.3, f32[512]{0:T(512)S(1)} %get-tuple-element.39, bf16[2,512,128]{2,1,0:T(8,128)(2,1)} %collective-permute-done.1), kind=kOutput, calls=%fused_computation.172 | convolution fusion | flops 67633152 | bytes 1443840 | tf_op jit(solution)/shard_map/dot_general | solution.py:82
  83.6 0.7 copy-done.22
  84.6 0.9 copy-done
  85.8 0.7 copy-done.9
  86.5 1.2 %fusion.124 = f32[512,128]{0,1:T(8,128)S(1)} fusion(f32[512,512]{0,1:T(8,128)S(1)} %copy-done, f32[512]{0:T(512)S(1)} %get-tuple-element.30, bf16[2,512,128]{2,1,0:T(8,128)(2,1)} %collective-permute-done.1), kind=kOutput, calls=%fused_computation.173 | convolution fusion | flops 67633152 | bytes 1443840 | tf_op jit(solution)/shard_map/dot_general | solution.py:82
  88.5 0.6 copy-done.21
  89.8 0.7 copy-done.8
  90.5 1.2 %fusion.130 = f32[512,128]{0,1:T(8,128)S(1)} fusion(f32[512,512]{0,1:T(8,128)S(1)} %get-tuple-element.94, f32[512]{0:T(512)S(1)} %get-tuple-element.21, bf16[2,512,128]{2,1,0:T(8,128)(2,1)} %collective-permute-done.1), kind=kOutput, calls=%fused_computation.174 | convolution fusion | flops 67633152 | bytes 1443840 | tf_op jit(solution)/shard_map/dot_general | solution.py:82
  92.1 1.2 %fusion.53 = f32[512,128]{0,1:T(8,128)S(1)} fusion(f32[512,128]{0,1:T(8,128)S(1)} %fusion.58, f32[512,512]{0,1:T(8,128)S(1)} %get-tuple-element.60, f32[512]{0:T(512)S(1)} %get-tuple-element.47, f32[512]{0:T(512)S(1)} %get-tuple-element.42, bf16[2,512,128]{2,1,0:T(8,128)(2,1)} %collective-permute-done.2), kind=kOutput, calls=%fused_computation.90 | convolution fusion | flops 67764224 | bytes 1708032 | tf_op jit(solution)/shard_map/dot_general | solution.py:82
  93.9 1.2 %fusion.49 = f32[512,128]{0,1:T(8,128)S(1)} fusion(f32[512,128]{0,1:T(8,128)S(1)} %fusion.60, f32[512,512]{0,1:T(8,128)S(1)} %get-tuple-element.70, f32[512]{0:T(512)S(1)} %get-tuple-element.38, f32[512]{0:T(512)S(1)} %get-tuple-element.33, bf16[2,512,128]{2,1,0:T(8,128)(2,1)} %collective-permute-done.2), kind=kOutput, calls=%fused_computation.86 | convolution fusion | flops 67764224 | bytes 1708032 | tf_op jit(solution)/shard_map/dot_general | solution.py:82
  95.8 1.2 %fusion.45 = f32[512,128]{0,1:T(8,128)S(1)} fusion(f32[512,128]{0,1:T(8,128)S(1)} %fusion.62, f32[512,512]{0,1:T(8,128)S(1)} %get-tuple-element.80, f32[512]{0:T(512)S(1)} %get-tuple-element.29, f32[512]{0:T(512)S(1)} %get-tuple-element.24, bf16[2,512,128]{2,1,0:T(8,128)(2,1)} %collective-permute-done.2), kind=kOutput, calls=%fused_computation.82 | convolution fusion | flops 67764224 | bytes 1708032 | tf_op jit(solution)/shard_map/dot_general | solution.py:82
  97.7 1.2 %fusion.41 = f32[512,128]{0,1:T(8,128)S(1)} fusion(f32[512,128]{0,1:T(8,128)S(1)} %fusion.64, f32[512,512]{0,1:T(8,128)S(1)} %get-tuple-element.90, f32[512]{0:T(512)S(1)} %get-tuple-element.20, f32[512]{0:T(512)S(1)} %get-tuple-element.15, bf16[2,512,128]{2,1,0:T(8,128)(2,1)} %collective-permute-done.2), kind=kOutput, calls=%fused_computation.78 | convolution fusion | flops 67764224 | bytes 1708032 | tf_op jit(solution)/shard_map/dot_general | solution.py:82
  99.7 1.0 copy.11
  100.7 0.7 copy.14
  (126 shorter events, 14.4 us)
Async XLA Ops:
  0.6 18.8 %collective-permute-start = (bf16[512,128]{1,0:T(8,128)(2,1)}, bf16[512,128]{1,0:T(8,128)(2,1)S(1)}, u32[]{:S(2)}, u32[]{:S(2)}) collective-permute-start(bf16[512,128]{1,0:T(8,128)(2,1)} %param.5), channel_id=1, source_target_pairs={{0,1},{1,0},{2,3},{3,2},{4,5},{5,4},{6,7},{7,6},{8,9},{9,8},{10,11... | collective-permute-start | bytes 393224 | tf_op jit(solution)/shard_map/ppermute | solution.py:14
  3.5 0.7 copy-start.25
  4.7 14.8 %copy-start.32 = (bf16[512,512]{1,0:T(8,128)(2,1)S(1)}, bf16[512,512]{1,0:T(8,128)(2,1)}, u32[]{:S(2)}) copy-start(bf16[512,512]{1,0:T(8,128)(2,1)} %param.4) | copy-start | bytes 1572868
  5.5 14.0 %copy-start.7 = (bf16[512,128]{1,0:T(8,128)(2,1)S(1)}, bf16[512,128]{1,0:T(8,128)(2,1)}, u32[]{:S(2)}) copy-start(bf16[512,128]{1,0:T(8,128)(2,1)} %param.5) | copy-start | bytes 393220
  5.5 42.8 %all-to-all-start = ((bf16[64,16,128]{2,1,0:T(8,128)(2,1)}), bf16[64,16,128]{2,1,0:T(8,128)(2,1)S(1)}, u32[]{:S(2)}, u32[]{:S(2)}) async-start(bf16[64,16,128]{2,1,0:T(8,128)(2,1)} %bitcast.33), calls=%async_computation | async-start | bytes 524288 | tf_op jit(solution)/shard_map/all_to_all | solution.py:41
  16.1 27.3 %copy-start.12 = (s32[512]{0:T(512)}, s32[512]{0:T(512)S(1)}, u32[]{:S(2)}) copy-start(s32[512]{0:T(512)S(1)} %iota_add_fusion.4) | copy-start | bytes 6148
  16.1 27.3 %copy-start.20 = (s32[512]{0:T(512)}, s32[512]{0:T(512)S(1)}, u32[]{:S(2)}) copy-start(s32[512]{0:T(512)S(1)} %iota_add_fusion.3) | copy-start | bytes 6148
  16.1 27.2 %copy-start.37 = (pred[512]{0:T(512)(128)(4,1)}, pred[512]{0:T(512)(128)(4,1)S(1)}, u32[]{:S(2)}) copy-start(pred[512]{0:T(512)(128)(4,1)S(1)} %broadcast_compare_fusion.3) | copy-start | bytes 1540
  16.1 2.6 %copy-start.14 = (s32[512]{0:T(512)}, s32[512]{0:T(512)S(1)}, u32[]{:S(2)}) copy-start(s32[512]{0:T(512)S(1)} %iota_add_fusion) | copy-start | bytes 6148
  16.7 2.1 %copy-start.16 = (s32[512]{0:T(512)}, s32[512]{0:T(512)S(1)}, u32[]{:S(2)}) copy-start(s32[512]{0:T(512)S(1)} %iota_add_fusion.1) | copy-start | bytes 6148
  17.2 1.5 %copy-start.18 = (s32[512]{0:T(512)}, s32[512]{0:T(512)S(1)}, u32[]{:S(2)}) copy-start(s32[512]{0:T(512)S(1)} %iota_add_fusion.2) | copy-start | bytes 6148
  17.8 0.7 copy-start.31
  19.5 26.8 %copy-start.27 = (s32[512]{0:T(512)}, s32[512]{0:T(512)S(1)}, u32[]{:S(2)}) copy-start(s32[512]{0:T(512)S(1)} %get-tuple-element.12) | copy-start | bytes 6148
  20.0 4.9 %copy-start.4 = (f32[512,512]{0,1:T(8,128)}, f32[512,512]{0,1:T(8,128)S(1)}, u32[]{:S(2)}) copy-start(f32[512,512]{0,1:T(8,128)S(1)} %get-tuple-element.62) | copy-start | bytes 3145732
  20.5 5.2 %copy-start.1 = (f32[512,512]{0,1:T(8,128)}, f32[512,512]{0,1:T(8,128)S(1)}, u32[]{:S(2)}) copy-start(f32[512,512]{0,1:T(8,128)S(1)} %get-tuple-element.72) | copy-start | bytes 3145732
  21.5 14.1 %collective-permute-start.1 = (bf16[2,512,128]{2,1,0:T(8,128)(2,1)S(1)}, bf16[2,512,128]{2,1,0:T(8,128)(2,1)}, u32[]{:S(2)}, u32[]{:S(2)}) collective-permute-start(bf16[2,512,128]{2,1,0:T(8,128)(2,1)S(1)} %pad_maximum_fusion.1), channel_id=1, source_target_pairs={{0,16},{16,32},{32,48},{48,64},{64,80},{80,96},{96,112},{112,128},... | collective-permute-start | bytes 786440 | tf_op jit(solution)/shard_map/ppermute | solution.py:20
  35.6 13.4 %collective-permute-start.2 = (bf16[2,512,128]{2,1,0:T(8,128)(2,1)}, bf16[2,512,128]{2,1,0:T(8,128)(2,1)}, u32[]{:S(2)}, u32[]{:S(2)}) collective-permute-start(bf16[2,512,128]{2,1,0:T(8,128)(2,1)} %collective-permute-done.1), channel_id=1, source_target_pairs={{0,16},{16,32},{32,48},{48,64},{64,80},{80,96},{96,112},{112,128},... | collective-permute-start | bytes 786440 | tf_op jit(solution)/shard_map/ppermute | solution.py:20
  48.3 2.6 %copy-start.36 = (pred[512]{0:T(512)(128)(4,1)S(1)}, pred[512]{0:T(512)(128)(4,1)}, u32[]{:S(2)}) copy-start(pred[512]{0:T(512)(128)(4,1)} %broadcast_compare_fusion.2) | copy-start | bytes 1540
  49.0 12.6 %collective-permute-start.3 = (bf16[2,512,128]{2,1,0:T(8,128)(2,1)}, bf16[2,512,128]{2,1,0:T(8,128)(2,1)S(1)}, u32[]{:S(2)}, u32[]{:S(2)}) collective-permute-start(bf16[2,512,128]{2,1,0:T(8,128)(2,1)} %collective-permute-done.2), channel_id=1, source_target_pairs={{0,16},{16,32},{32,48},{48,64},{64,80},{80,96},{96,112},{112,128},... | collective-permute-start | bytes 786440 | tf_op jit(solution)/shard_map/ppermute | solution.py:20
  50.9 1.6 %copy-start.13 = (s32[512]{0:T(512)S(1)}, s32[512]{0:T(512)}, u32[]{:S(2)}) copy-start(s32[512]{0:T(512)} %copy-done.12) | copy-start | bytes 6148
  50.9 1.6 %copy-start.19 = (s32[512]{0:T(512)S(1)}, s32[512]{0:T(512)}, u32[]{:S(2)}) copy-start(s32[512]{0:T(512)} %copy-done.18) | copy-start | bytes 6148
  50.9 1.6 %copy-start.28 = (s32[512]{0:T(512)S(1)}, s32[512]{0:T(512)}, u32[]{:S(2)}) copy-start(s32[512]{0:T(512)} %copy-done.27) | copy-start | bytes 6148
  50.9 1.6 %copy-start.30 = (s32[512]{0:T(512)S(1)}, s32[512]{0:T(512)}, u32[]{:S(2)}) copy-start(s32[512]{0:T(512)} %get-tuple-element.10) | copy-start | bytes 6148
  50.9 1.6 %copy-start.33 = (bf16[512,512]{1,0:T(8,128)(2,1)S(1)}, bf16[512,512]{1,0:T(8,128)(2,1)}, u32[]{:S(2)}) copy-start(bf16[512,512]{1,0:T(8,128)(2,1)} %param.4) | copy-start | bytes 1572868
  55.3 8.4 %copy-start.17 = (s32[512]{0:T(512)S(1)}, s32[512]{0:T(512)}, u32[]{:S(2)}) copy-start(s32[512]{0:T(512)} %copy-done.16) | copy-start | bytes 6148
  55.3 8.4 %copy-start.29 = (s32[512]{0:T(512)S(1)}, s32[512]{0:T(512)}, u32[]{:S(2)}) copy-start(s32[512]{0:T(512)} %get-tuple-element.11) | copy-start | bytes 6148
  56.7 7.0 %copy-start.35 = (pred[512]{0:T(512)(128)(4,1)S(1)}, pred[512]{0:T(512)(128)(4,1)}, u32[]{:S(2)}) copy-start(pred[512]{0:T(512)(128)(4,1)} %broadcast_compare_fusion.1) | copy-start | bytes 1540
  61.6 12.2 %collective-permute-start.4 = (bf16[2,512,128]{2,1,0:T(8,128)(2,1)S(1)}, bf16[2,512,128]{2,1,0:T(8,128)(2,1)S(1)}, u32[]{:S(2)}, u32[]{:S(2)}) collective-permute-start(bf16[2,512,128]{2,1,0:T(8,128)(2,1)S(1)} %collective-permute-done.3), channel_id=1, source_target_pairs={{0,16},{16,32},{32,48},{48,64},{64,80},{80,96},{96,112},{112,128},... | collective-permute-start | bytes 786440 | tf_op jit(solution)/shard_map/ppermute | solution.py:20
  65.2 8.6 %copy-start.15 = (s32[512]{0:T(512)S(1)}, s32[512]{0:T(512)}, u32[]{:S(2)}) copy-start(s32[512]{0:T(512)} %copy-done.14) | copy-start | bytes 6148
  65.2 8.6 %copy-start.26 = (s32[512]{0:T(512)S(1)}, s32[512]{0:T(512)}, u32[]{:S(2)}) copy-start(s32[512]{0:T(512)} %get-tuple-element.8) | copy-start | bytes 6148
  65.7 8.1 %copy-start.34 = (pred[512]{0:T(512)(128)(4,1)S(1)}, pred[512]{0:T(512)(128)(4,1)}, u32[]{:S(2)}) copy-start(pred[512]{0:T(512)(128)(4,1)} %broadcast_compare_fusion) | copy-start | bytes 1540
  74.3 0.7 copy-start.24
  74.9 1.2 %copy-start.6 = (f32[512,512]{0,1:T(8,128)S(1)}, f32[512,512]{0,1:T(8,128)}, u32[]{:S(2)}) copy-start(f32[512,512]{0,1:T(8,128)} %get-tuple-element.64) | copy-start | bytes 3145732
  76.2 0.7 copy-start.11
  76.5 1.6 %copy-start.5 = (f32[512,512]{0,1:T(8,128)S(1)}, f32[512,512]{0,1:T(8,128)}, u32[]{:S(2)}) copy-start(f32[512,512]{0,1:T(8,128)} %copy-done.4) | copy-start | bytes 3145732
  78.9 0.7 copy-start.23
  79.6 1.2 %copy-start.3 = (f32[512,512]{0,1:T(8,128)S(1)}, f32[512,512]{0,1:T(8,128)}, u32[]{:S(2)}) copy-start(f32[512,512]{0,1:T(8,128)} %get-tuple-element.74) | copy-start | bytes 3145732
  80.8 0.7 copy-start.10
  81.1 1.6 %copy-start.2 = (f32[512,512]{0,1:T(8,128)S(1)}, f32[512,512]{0,1:T(8,128)}, u32[]{:S(2)}) copy-start(f32[512,512]{0,1:T(8,128)} %copy-done.1) | copy-start | bytes 3145732
  83.6 0.7 copy-start.22
  84.3 1.2 %copy-start = (f32[512,512]{0,1:T(8,128)S(1)}, f32[512,512]{0,1:T(8,128)}, u32[]{:S(2)}) copy-start(f32[512,512]{0,1:T(8,128)} %get-tuple-element.84) | copy-start | bytes 3145732
  85.8 0.7 copy-start.9
  88.5 0.6 copy-start.21
  89.8 0.7 copy-start.8
where the time goes:
time: 102 us; the launch traced here: 101 us
  matrix products  36.1 us (35%)
  starting transfers between devices  21.8 us (21%)
  waiting for transfers between devices  21.2 us (21%)
  local copies, waits for them, and re-layouts  12.4 us (12%)
  other arithmetic  8.61 us (8%)
  between operations  1.32 us (1%)
    dot_general x20, matrix products, attend(): lax.dot_general(head_queries[head_index], kv_block[0], (((1,), (1,)), (()...  22.2 us
    ppermute x4, waiting for transfers between devices, passed_along(): lax.ppermute(value, axis, [(source, source + steps) for source in range(l...  21.2 us
    dot_general x20, matrix products, attend(): jnp.dot(weights.astype(jnp.bfloat16), kv_block[1], preferred_element_type...  13.7 us
    unnamed x79, local copies, waits for them, and re-layouts  11.3 us
    all_to_all x1, starting transfers between devices, hand_over(): lax.all_to_all(outgoing, 'ctx', split_axis=0, concat_axis=0, tiled=True)  10.6 us
    ppermute x4, starting transfers between devices, passed_along(): lax.ppermute(value, axis, [(source, source + steps) for source in range(l...  9.28 us
    reduce_sum x12, other arithmetic, attend(): jnp.sum(weights, axis=1)  5.55 us
  transfers between devices with their start and end apart: 6, of which 4 were waited for; matrix products, arithmetic and copies ran while one was open for 28% of the time, Pallas kernels for 0%

commit v1 on v0

v1 whole, which is shorter than its diff:
```python
import functools
import math

import jax
import jax.numpy as jnp
from jax import lax
from jax.experimental import pallas as pl
from jax.experimental.pallas import tpu as pltpu
from jax.sharding import PartitionSpec as P

SPAN = 4
PAGE = 16
CAP = 2
Y = 4
CHUNKS = 2
BIG = float(2**20)
MESH = pl.DeviceIdType.MESH


def kernel(
    n_ctx, n_docs, q_ref, kv_ref, len_ref, owner_ref, att_ref, cache_ref,
    win, kaug, qaug, acc, top, outgoing,
    recv_direct, recv_partner, send_y, send_z, send_partner, recv_page, send_page, own_page,
):
    tok, hd = kv_ref.shape
    heads = q_ref.shape[1] // hd
    pages = owner_ref.shape[0]
    rows_per_owner = CAP * PAGE
    chunk = tok // CHUNKS
    scale = hd ** (-0.5) * math.log2(math.e)

    c = lax.axis_index("ctx")
    g = lax.axis_index("grp")
    a = lax.rem(c, Y)
    kind = lax.rem(g, 2)
    partner = g + 1 - 2 * kind

    barrier = pltpu.get_barrier_semaphore()

    def greet(k, carry):
        pl.semaphore_signal(barrier, inc=1, device_id=(lax.rem(c + k, n_ctx), g), device_id_type=MESH)
        return carry

    pl.semaphore_signal(barrier, inc=1, device_id=(c, partner), device_id_type=MESH)
    lax.fori_loop(1, n_ctx, greet, 0)

    win[kind, 0] = kv_ref[...]

    lane = lax.broadcasted_iota(jnp.int32, (1, hd), 1)
    starts = jnp.where(lane == n_docs, -(2**30), 2**30)
    ends = jnp.where(lane == n_docs, 0, -(2**30))
    total = jnp.int32(0)
    for doc in range(n_docs):
        starts = jnp.where(lane == doc, total, starts)
        total = total + len_ref[doc]
        ends = jnp.where(lane == doc, total, ends)
    row = lax.broadcasted_iota(jnp.int32, (tok, hd), 0)

    def in_doc(d):
        pos = row + (c - d) * tok
        return (pos >= starts) & (pos < ends)

    for d in range(SPAN + 1):
        kaug[d] = jnp.where(in_doc(d), 1.0, 0.0).astype(jnp.bfloat16)
    qaug[...] = jnp.where(in_doc(0) | (lane > n_docs), 0.0, -BIG).astype(jnp.bfloat16)

    col = lax.broadcasted_iota(jnp.int32, (pages, tok), 1)
    page = lax.broadcasted_iota(jnp.int32, (pages, tok), 0)
    owners = jnp.broadcast_to(owner_ref[...], (pages, tok))
    mine = jnp.sum(jnp.where(page == col // PAGE, owners, 0), axis=0, keepdims=True)
    rank = jnp.sum(
        jnp.where((owners == mine) & (page < col // PAGE), 1, 0), axis=0, keepdims=True
    )
    target = (mine * CAP + rank) * PAGE + lax.rem(col[:1], PAGE)
    part = 256
    for r0 in range(0, n_ctx * rows_per_owner, part):
        out_row = lax.broadcasted_iota(jnp.int32, (part, tok), 0) + r0
        pick = jnp.where(out_row == target, 1.0, 0.0).astype(jnp.bfloat16)
        outgoing[r0 : r0 + part, :] = jnp.dot(
            pick, kv_ref[...], preferred_element_type=jnp.float32
        ).astype(jnp.bfloat16)

    pl.semaphore_wait(barrier, n_ctx)

    def part_of(k, d, i):
        return win.at[k, d, pl.ds(i * chunk, chunk), :]

    def to_partner(d, i):
        return pltpu.make_async_remote_copy(
            src_ref=part_of(kind, d, i), dst_ref=part_of(kind, d, i),
            send_sem=send_partner.at[d, i], recv_sem=recv_partner.at[d, i],
            device_id=(c, partner), device_id_type=MESH,
        )

    def from_partner(d, i):
        return pltpu.make_async_remote_copy(
            src_ref=part_of(1 - kind, d, i), dst_ref=part_of(1 - kind, d, i),
            send_sem=send_partner.at[d, i], recv_sem=recv_partner.at[d, i],
            device_id=(c, partner), device_id_type=MESH,
        )

    def along_z(i):
        return pltpu.make_async_remote_copy(
            src_ref=part_of(kind, 0, i), dst_ref=part_of(kind, SPAN, i),
            send_sem=send_z.at[i], recv_sem=recv_direct.at[SPAN, i],
            device_id=(lax.rem(c + Y, n_ctx), g), device_id_type=MESH,
        )

    def along_y(d, i):
        step = jnp.where(d <= a, 1, -1)
        return pltpu.make_async_remote_copy(
            src_ref=part_of(kind, d, i), dst_ref=part_of(kind, d + step, i),
            send_sem=send_y.at[d, i], recv_sem=recv_direct.at[d + step, i],
            device_id=(c + step, g), device_id_type=MESH,
        )

    def goes_on(d):
        return jnp.where(d <= a, a < Y - 1, a > 0)

    def forward(d):
        for i in range(CHUNKS):
            pltpu.make_async_remote_copy(
                src_ref=part_of(kind, d, i), dst_ref=part_of(kind, d, i),
                send_sem=send_y.at[d, i], recv_sem=recv_direct.at[d, i],
                device_id=(c, partner), device_id_type=MESH,
            ).wait_recv()

            @pl.when(goes_on(d))
            def _():
                along_y(d, i).start()

            to_partner(d, i).start()

    def arrive(d):
        for i in range(CHUNKS):
            from_partner(d, i).wait_recv()

    for i in range(CHUNKS):
        along_z(i).start()

        @pl.when(a < Y - 1)
        def _():
            along_y(jnp.int32(0), i).start()

        to_partner(0, i).start()

    def page_copy(k):
        peer = lax.rem(c + k, n_ctx)
        return pltpu.make_async_remote_copy(
            src_ref=outgoing.at[pl.ds(peer * rows_per_owner, rows_per_owner), :],
            dst_ref=cache_ref.at[pl.ds(c * rows_per_owner, rows_per_owner), :],
            send_sem=send_page.at[k], recv_sem=recv_page.at[k],
            device_id=(peer, g), device_id_type=MESH,
        )

    def send_pages(k0, k1):
        def body(k, carry):
            page_copy(k).start()
            return carry

        lax.fori_loop(k0, k1, body, 0)

    own = pltpu.make_async_copy(
        outgoing.at[pl.ds(c * rows_per_owner, rows_per_owner), :],
        cache_ref.at[pl.ds(c * rows_per_owner, rows_per_owner), :],
        own_page,
    )
    own.start()

    ones = jnp.ones((tok, hd), jnp.bfloat16)

    def unit(d, head, r0, nr, k0, nk, causal, first, last):
        rows = slice(r0, r0 + nr)
        query = jnp.concatenate([q_ref[rows, head * hd : (head + 1) * hd], qaug[rows, :]], axis=1)
        key = jnp.concatenate([win[0, d, k0 : k0 + nk, :], kaug[d, k0 : k0 + nk, :]], axis=1)
        value = jnp.concatenate([win[1, d, k0 : k0 + nk, :], ones[:nk]], axis=1)
        scores = lax.dot_general(
            query, key, (((1,), (1,)), ((), ())), preferred_element_type=jnp.float32
        )
        if causal:
            q_pos = lax.broadcasted_iota(jnp.int32, (nr, nk), 0) + r0
            k_pos = lax.broadcasted_iota(jnp.int32, (nr, nk), 1) + k0
            scores = jnp.where(k_pos <= q_pos, scores, -BIG)
        peak = jnp.max(scores, axis=1, keepdims=True)
        if first:
            new = jnp.broadcast_to(peak, (nr, hd))
        else:
            old = top[head, rows, :]
            new = jnp.maximum(old, peak)
        wide = jnp.concatenate([new] * (nk // hd), axis=1)
        weights = jnp.exp2((scores - wide) * scale).astype(jnp.bfloat16)
        product = jnp.dot(weights, value, preferred_element_type=jnp.float32)
        if not first:
            fade = jnp.exp2((old - new) * scale)
            product = acc[head, rows, :] * jnp.concatenate([fade, fade], axis=1) + product
        if last:
            att_ref[rows, head * hd : (head + 1) * hd] = (
                product[:, :hd] / product[:, hd:]
            ).astype(jnp.bfloat16)
        else:
            acc[head, rows, :] = product
            top[head, rows, :] = new

    half = tok // 2
    arrive(0)
    for head in range(heads):
        unit(0, head, 0, half, 0, half, True, True, False)
        unit(0, head, half, half, 0, tok, True, True, False)

    forward(SPAN)
    d1 = jnp.where(a == 0, 3, 1)
    d2 = jnp.where(a == 0, 2, jnp.where(a == Y - 1, 2, 3))
    d3 = 6 - d1 - d2
    forward(d1)
    send_pages(1, n_ctx)
    arrive(SPAN)
    for head in range(heads):
        unit(SPAN, head, 0, half, 0, tok, False, False, False)
        unit(SPAN, head, half, half, half, half, False, False, False)
    for at, d in enumerate((d1, d2, d3)):
        if at > 0:
            forward(d)
        arrive(d)
        for head in range(heads):
            for r0 in (0, half):
                unit(d, head, r0, half, 0, tok, False, False, at == 2)

    for i in range(CHUNKS):
        along_z(i).wait_send()
        for d in range(SPAN + 1):
            to_partner(d, i).wait_send()

            @pl.when(goes_on(d))
            def _():
                along_y(jnp.int32(d), i).wait_send()

    def pages_done(k, carry):
        copy = page_copy(k)
        copy.wait_send()
        copy.wait_recv()
        return carry

    lax.fori_loop(1, n_ctx, pages_done, 0)
    own.wait()


def per_device(n_ctx, queries, kv_cols, lengths, page_owner):
    tok, hd = kv_cols.shape
    heads = queries.shape[1] // hd
    slots = n_ctx * CAP * PAGE
    bf16, f32 = jnp.bfloat16, jnp.float32
    vmem = pl.BlockSpec(memory_space=pltpu.VMEM)
    smem = pl.BlockSpec(memory_space=pltpu.SMEM)
    dma = pltpu.SemaphoreType.DMA
    attended, cache = pl.pallas_call(
        functools.partial(kernel, n_ctx, lengths.shape[0]),
        out_shape=(
            jax.ShapeDtypeStruct(queries.shape, bf16),
            jax.ShapeDtypeStruct((slots, hd), bf16),
        ),
        in_specs=[vmem, vmem, smem, vmem],
        out_specs=(vmem, vmem),
        scratch_shapes=[
            pltpu.VMEM((2, SPAN + 1, tok, hd), bf16),
            pltpu.VMEM((SPAN + 1, tok, hd), bf16),
            pltpu.VMEM((tok, hd), bf16),
            pltpu.VMEM((heads, tok, 2 * hd), f32),
            pltpu.VMEM((heads, tok, hd), f32),
            pltpu.VMEM((slots, hd), bf16),
            dma((SPAN + 1, CHUNKS)),
            dma((SPAN + 1, CHUNKS)),
            dma((SPAN + 1, CHUNKS)),
            dma((CHUNKS,)),
            dma((SPAN + 1, CHUNKS)),
            dma((n_ctx,)),
            dma((n_ctx,)),
            dma(()),
        ],
        compiler_params=pltpu.CompilerParams(
            collective_id=0, has_side_effects=True, vmem_limit_bytes=48 * 2**20
        ),
        cost_estimate=pl.CostEstimate(
            flops=4 * tok * heads * tok * SPAN * hd,
            bytes_accessed=4 * tok * heads * hd,
            transcendentals=tok * heads * tok * SPAN,
        ),
    )(queries, kv_cols, lengths, page_owner)
    return attended, cache.reshape(n_ctx * CAP, PAGE, hd)


def solution(mesh):
    in_specs = (P("ctx", "grp"), P("ctx", "grp"), P(), P("ctx", None))
    out_specs = (P("ctx", "grp"), P("ctx", None, "grp"))
    return jax.shard_map(
        functools.partial(per_device, mesh.shape["ctx"]),
        mesh=mesh, in_specs=in_specs, out_specs=out_specs, check_vma=False,
    )
```

time: 102 us -> 42.4 us (0.42)
  the two profiles are of different devices: /device:TPU:258 before, /device:TPU:1 now
where the time goes in v1:
time: 42.4 us; the launch traced here: 42.2 us
  Pallas kernels  37.3 us (88%)
  local copies, waits for them, and re-layouts  4.19 us (10%)
  between operations  0.65 us (2%)
    pallas_call x1, Pallas kernels, per_device(): pl.pallas_call(functools.partial(kernel, n_ctx, lengths.shape[0]), out_sh...  37.3 us
    unnamed x9, local copies, waits for them, and re-layouts  4.19 us

profile of v1, /device:TPU:1, one launch (start us, length us, event | category | flops | bytes accessed | tf_op | source)
XLA Modules:
  0.0 42.2 jit_solution(8887767959650039984)
XLA Ops:
  0.6 0.0 copy-start.2
  0.6 0.7 %copy.6.owner_ref = s32[32,1]{1,0:T(8,128)S(1)} copy(s32[32,1]{0,1:T(1,128)} %param.7) | data formatting | bytes 256 | tf_op args[3]
  1.4 0.0 copy-done.2
  1.4 0.0 copy-start
  1.4 1.0 %copy-done = bf16[512,512]{1,0:T(8,128)(2,1)S(1)} copy-done((bf16[512,512]{1,0:T(8,128)(2,1)S(1)}, bf16[512,512]{1,0:T(8,128)(2,1)}, u32[]{:S(2)}) %copy-start) | copy-done | bytes 524312
  2.4 0.0 copy-start.1
  2.4 0.9 %copy-done.1 = bf16[512,128]{1,0:T(8,128)(2,1)S(1)} copy-done((bf16[512,128]{1,0:T(8,128)(2,1)S(1)}, bf16[512,128]{1,0:T(8,128)(2,1)}, u32[]{:S(2)}) %copy-start.1) | copy-done | bytes 131096
  3.3 37.3 %shard_map.59 = (bf16[512,512]{1,0:T(8,128)(2,1)S(1)}, bf16[1024,128]{1,0:T(8,128)(2,1)S(1)}) custom-call(bf16[512,512]{1,0:T(8,128)(2,1)S(1)} %copy-done, bf16[512,128]{1,0:T(8,128)(2,1)S(1)} %copy-done.1, s32[16]{0:T(128)S(1)} %copy-done.2, s32[32,1]{1,0:T(8,128)S(1)} %copy.6.owner_ref), custom_call_target="tpu_custom_call" | custom-call | flops 2147483648 | bytes 1048576 | tf_op jit(solution)/shard_map/pallas_call | solution.py:255
  40.7 0.8 %copy.9 = bf16[512,512]{1,0:T(8,128)(2,1)} copy(bf16[512,512]{1,0:T(8,128)(2,1)S(1)} %get-tuple-element.8) | data formatting | bytes 1048576
  41.5 0.7 %copy.10 = bf16[64,16,128]{2,1,0:T(8,128)(2,1)} copy(bf16[64,16,128]{2,1,0:T(8,128)(2,1)S(1)} %bitcast.1) | data formatting | bytes 524288
Async XLA Ops:
  0.6 0.8 %copy-start.2 = (s32[16]{0:T(128)S(1)}, s32[16]{0:T(128)}, u32[]{:S(2)}) copy-start(s32[16]{0:T(128)} %len_ref.1) | copy-start | bytes 196
  1.4 1.0 %copy-start = (bf16[512,512]{1,0:T(8,128)(2,1)S(1)}, bf16[512,512]{1,0:T(8,128)(2,1)}, u32[]{:S(2)}) copy-start(bf16[512,512]{1,0:T(8,128)(2,1)} %q_ref.1) | copy-start | bytes 1572868
  2.4 0.9 %copy-start.1 = (bf16[512,128]{1,0:T(8,128)(2,1)S(1)}, bf16[512,128]{1,0:T(8,128)(2,1)}, u32[]{:S(2)}) copy-start(bf16[512,128]{1,0:T(8,128)(2,1)} %kv_ref.1) | copy-start | bytes 393220

commit v2 on v1

v2 whole, which is shorter than its diff:
```python
import functools
import math

import jax
import jax.numpy as jnp
from jax import lax
from jax.experimental import pallas as pl
from jax.experimental.pallas import tpu as pltpu
from jax.sharding import PartitionSpec as P

SPAN = 4
PAGE = 16
CAP = 2
Y = 4
CHUNKS = 4
WINDOW = 4
BIG = float(2**20)
MESH = pl.DeviceIdType.MESH


def kernel(
    n_ctx, n_docs, q_hbm, kv_hbm, len_hbm, owner_hbm, att_ref, cache_ref,
    win, far, kaug, qaug, acc, top, outgoing, q_ref, owner_ref, len_ref,
    recv_direct, recv_partner, send_own, send_on, send_partner, recv_page, send_page,
    own_page, load,
):
    tok, hd = kv_hbm.shape
    heads = q_hbm.shape[1] // hd
    pages = owner_hbm.shape[1]
    rows_per_owner = CAP * PAGE
    chunk = tok // CHUNKS
    scale = hd ** (-0.5) * math.log2(math.e)

    c = lax.axis_index("ctx")
    g = lax.axis_index("grp")
    a = lax.rem(c, Y)
    z = c // Y
    top_z = n_ctx // Y - 1
    row0 = z * Y
    kind = lax.rem(g, 2)
    partner = g + 1 - 2 * kind

    load_kv = pltpu.make_async_copy(kv_hbm, win.at[kind], load.at[0])
    load_owner = pltpu.make_async_copy(owner_hbm, owner_ref, load.at[1])
    load_len = pltpu.make_async_copy(len_hbm, len_ref, load.at[2])
    load_q = pltpu.make_async_copy(q_hbm, q_ref, load.at[3])
    load_kv.start()
    load_owner.start()
    load_len.start()
    load_q.start()

    barrier = pltpu.get_barrier_semaphore()

    def signal(semaphore, ctx, grp):
        pl.semaphore_signal(semaphore, inc=1, device_id=(ctx, grp), device_id_type=MESH)

    signal(barrier, c, partner)
    for k in range(1, Y):
        signal(barrier, row0 + lax.rem(a + k, Y), g)

    @pl.when(z > 0)
    def _():
        for k in range(Y):
            pl.when(a <= k)(functools.partial(signal, barrier, row0 - Y + k, g))

    def tell(p, carry):
        signal(barrier, p, g)
        return carry

    lax.fori_loop(row0 + Y, n_ctx, tell, 0)
    load_owner.wait()
    own = jnp.broadcast_to(owner_ref[...], (pages, pages))
    k_page = lax.broadcasted_iota(jnp.int32, (pages, pages), 0)
    i_page = lax.broadcasted_iota(jnp.int32, (pages, pages), 1)
    own_col = jnp.sum(jnp.where(k_page == i_page, own, 0), axis=1, keepdims=True)
    rank = jnp.sum(jnp.where((own_col == own) & (k_page < i_page), 1, 0), axis=0, keepdims=True)
    slot = (owner_ref[...] * CAP + rank).astype(jnp.bfloat16)
    col = lax.broadcasted_iota(jnp.int32, (pages, tok), 1)
    spread = jnp.where(
        lax.broadcasted_iota(jnp.int32, (pages, tok), 0) == col // PAGE, 1.0, 0.0
    ).astype(jnp.bfloat16)
    slot_of = jnp.dot(
        jnp.broadcast_to(slot, (16, pages)), spread, preferred_element_type=jnp.float32
    )[:1]
    target = slot_of.astype(jnp.int32) * PAGE + lax.rem(col[:1], PAGE)
    load_kv.wait()
    part = 256
    for r0 in range(0, n_ctx * rows_per_owner, part):
        out_row = lax.broadcasted_iota(jnp.int32, (part, tok), 0) + r0
        pick = jnp.where(out_row == target, 1.0, 0.0).astype(jnp.bfloat16)
        outgoing[r0 : r0 + part, :] = jnp.dot(
            pick, win[kind], preferred_element_type=jnp.float32
        ).astype(jnp.bfloat16)

    pl.semaphore_wait(barrier, Y + row0 + jnp.where(z < top_z, a + 1, 0))

    def own_chunk(i):
        return win.at[kind, pl.ds(i * chunk, chunk), :]

    def ahead(d, i):
        return pltpu.make_async_remote_copy(
            src_ref=own_chunk(i), dst_ref=far.at[kind, i, d - 1],
            send_sem=send_own.at[d, i], recv_sem=recv_direct.at[d, i],
            device_id=(c + d, g), device_id_type=MESH,
        )

    def is_ahead(d):
        far_off = (a == 0) if d == 3 else (a == Y - 1) if d == 1 else False
        return (c + d < n_ctx) & jnp.logical_not(far_off)

    def onward(i):
        step = jnp.where(a == 2, 1, -1)
        return pltpu.make_async_remote_copy(
            src_ref=far.at[kind, i, 1], dst_ref=far.at[kind, i, 1 + step],
            send_sem=send_on.at[i], recv_sem=recv_direct.at[2 + step, i],
            device_id=(c + step, g), device_id_type=MESH,
        )

    goes_on = (a == 2) | ((a == 1) & (z > 0))

    def own_to_partner(k):
        return pltpu.make_async_remote_copy(
            src_ref=win.at[k], dst_ref=win.at[k],
            send_sem=send_partner.at[CHUNKS], recv_sem=recv_partner.at[CHUNKS],
            device_id=(c, partner), device_id_type=MESH,
        )

    def far_to_partner(k, i):
        return pltpu.make_async_remote_copy(
            src_ref=far.at[k, i], dst_ref=far.at[k, i],
            send_sem=send_partner.at[i], recv_sem=recv_partner.at[i],
            device_id=(c, partner), device_id_type=MESH,
        )

    def came(d, i):
        return pltpu.make_async_remote_copy(
            src_ref=far.at[kind, i, d - 1], dst_ref=far.at[kind, i, d - 1],
            send_sem=send_own.at[d, i], recv_sem=recv_direct.at[d, i],
            device_id=(c, partner), device_id_type=MESH,
        )

    def receive(i):
        for d in (2, 1, 3, 4):
            pl.when(c >= d)(came(d, i).wait_recv)
            if d == 2:
                pl.when(goes_on)(onward(i).start)
        far_to_partner(kind, i).start()

    def send(i):
        for d in (2, 1, 3, 4):
            pl.when(is_ahead(d))(ahead(d, i).start)

    for i in range(WINDOW):
        send(i)
    own_to_partner(kind).start()

    def slots_of(p):
        return pl.ds(p * rows_per_owner, rows_per_owner)

    def page_to(p):
        return pltpu.make_async_remote_copy(
            src_ref=outgoing.at[slots_of(p), :], dst_ref=cache_ref.at[slots_of(c), :],
            send_sem=send_page.at[p], recv_sem=recv_page.at[c],
            device_id=(p, g), device_id_type=MESH,
        )

    def page_from(p):
        return pltpu.make_async_remote_copy(
            src_ref=outgoing.at[slots_of(p), :], dst_ref=cache_ref.at[slots_of(p), :],
            send_sem=send_page.at[p], recv_sem=recv_page.at[p],
            device_id=(p, g), device_id_type=MESH,
        )

    def others(first, last, act):
        def body(p, carry):
            pl.when(p != c)(functools.partial(act, p))
            return carry

        lax.fori_loop(first, last, body, 0)

    own_pages = pltpu.make_async_copy(
        outgoing.at[slots_of(c), :], cache_ref.at[slots_of(c), :], own_page
    )
    own_pages.start()

    others(0, row0 + Y, lambda p: page_to(p).start())

    load_len.wait()
    lane = lax.broadcasted_iota(jnp.int32, (1, hd), 1)
    starts = jnp.where(lane == n_docs, -(2**30), 2**30)
    ends = jnp.where(lane == n_docs, 0, -(2**30))
    total = jnp.int32(0)
    for doc in range(n_docs):
        starts = jnp.where(lane == doc, total, starts)
        total = total + len_ref[doc]
        ends = jnp.where(lane == doc, total, ends)
    row = lax.broadcasted_iota(jnp.int32, (tok, hd), 0)

    def in_doc(pos):
        return (pos >= starts) & (pos < ends)

    def one_in_doc(pos):
        return jnp.where(in_doc(pos), 1.0, 0.0).astype(jnp.bfloat16)

    here = row + c * tok
    kaug[CHUNKS] = one_in_doc(here)
    for i in range(CHUNKS):
        kaug[i] = one_in_doc((c - 1 - row // chunk) * tok + i * chunk + lax.rem(row, chunk))
    qaug[...] = jnp.where(in_doc(here) | (lane > n_docs), 0.0, -BIG).astype(jnp.bfloat16)

    for d in range(1, SPAN + 1):

        @pl.when(c < d)
        def _():
            for i in range(CHUNKS):
                far[kind, i, d - 1] = jnp.zeros((chunk, hd), jnp.bfloat16)

    load_q.wait()

    ones = jnp.ones((tok, hd), jnp.bfloat16)

    def unit(keys, values, tags, head, r0, nr, k0, causal, first, last):
        nk = keys.shape[0]
        rows = slice(r0, r0 + nr)
        query = jnp.concatenate([q_ref[rows, head * hd : (head + 1) * hd], qaug[rows, :]], axis=1)
        key = jnp.concatenate([keys, tags], axis=1)
        value = jnp.concatenate([values, ones[:nk]], axis=1)
        scores = lax.dot_general(
            query, key, (((1,), (1,)), ((), ())), preferred_element_type=jnp.float32
        )
        if causal:
            q_pos = lax.broadcasted_iota(jnp.int32, (nr, nk), 0) + r0
            k_pos = lax.broadcasted_iota(jnp.int32, (nr, nk), 1) + k0
            scores = jnp.where(k_pos <= q_pos, scores, -BIG)
        peak = jnp.max(scores, axis=1, keepdims=True)
        if first:
            new = jnp.broadcast_to(peak, (nr, hd))
        else:
            old = top[head, rows, :]
            new = jnp.maximum(old, peak)
        wide = jnp.concatenate([new] * (nk // hd), axis=1)
        weights = jnp.exp2((scores - wide) * scale).astype(jnp.bfloat16)
        product = jnp.dot(weights, value, preferred_element_type=jnp.float32)
        if not first:
            fade = jnp.exp2((old - new) * scale)
            product = acc[head, rows, :] * jnp.concatenate([fade, fade], axis=1) + product
        if last:
            att_ref[rows, head * hd : (head + 1) * hd] = (
                product[:, :hd] / product[:, hd:]
            ).astype(jnp.bfloat16)
        else:
            acc[head, rows, :] = product
            top[head, rows, :] = new

    half = tok // 2

    def diagonal(head):
        for r0, nk in ((0, half), (half, tok)):
            unit(win[0, :nk], win[1, :nk], kaug[CHUNKS, :nk], head, r0, half, 0, True, True, False)

    def earlier(i, head):
        for r0 in (0, half):
            near = SPAN if (i + 1) * chunk > r0 + 1 else SPAN - 1
            keys, values = (
                far[k, i, :near].reshape(near * chunk, hd) for k in range(2)
            )
            tags = kaug[i, : near * chunk]
            unit(keys, values, tags, head, r0, half, 0, False, False, i == CHUNKS - 1)

    own_to_partner(1 - kind).wait_recv()
    for head in range(heads):
        diagonal(head)
    receive(0)
    for i in range(CHUNKS):
        far_to_partner(1 - kind, i).wait_recv()
        for head in range(heads):
            if head == heads // 2 and i + 1 < CHUNKS:
                if i + WINDOW < CHUNKS:
                    send(i + WINDOW)
                receive(i + 1)
            earlier(i, head)

    def answer(p):
        page_from(p).wait_recv()
        page_to(p).start()

    others(row0 + Y, n_ctx, answer)

    own_to_partner(kind).wait_send()
    for i in range(CHUNKS):
        far_to_partner(kind, i).wait_send()
        for d in range(1, SPAN + 1):
            pl.when(is_ahead(d))(ahead(d, i).wait_send)
        pl.when(goes_on)(onward(i).wait_send)
    others(0, row0 + Y, lambda p: page_from(p).wait_recv())
    others(0, n_ctx, lambda p: page_to(p).wait_send())
    own_pages.wait()


def per_device(n_ctx, queries, kv_cols, lengths, page_owner):
    tok, hd = kv_cols.shape
    heads = queries.shape[1] // hd
    slots = n_ctx * CAP * PAGE
    bf16, f32 = jnp.bfloat16, jnp.float32
    vmem = pl.BlockSpec(memory_space=pltpu.VMEM)
    hbm = pl.BlockSpec(memory_space=pltpu.HBM)
    dma = pltpu.SemaphoreType.DMA
    attended, cache = pl.pallas_call(
        functools.partial(kernel, n_ctx, lengths.shape[0]),
        out_shape=(pltpu.VMEM(queries.shape, bf16), pltpu.VMEM((slots, hd), bf16)),
        in_specs=[hbm] * 4,
        out_specs=(vmem, vmem),
        scratch_shapes=[
            pltpu.VMEM((2, tok, hd), bf16),
            pltpu.VMEM((2, CHUNKS, SPAN, tok // CHUNKS, hd), bf16),
            pltpu.VMEM((CHUNKS + 1, tok, hd), bf16),
            pltpu.VMEM((tok, hd), bf16),
            pltpu.VMEM((heads, tok, 2 * hd), f32),
            pltpu.VMEM((heads, tok, hd), f32),
            pltpu.VMEM((slots, hd), bf16),
            pltpu.VMEM(queries.shape, bf16),
            pltpu.VMEM((1, page_owner.shape[0]), jnp.int32),
            pltpu.SMEM(lengths.shape, jnp.int32),
            dma((SPAN + 1, CHUNKS)),
            dma((CHUNKS + 1,)),
            dma((SPAN + 1, CHUNKS)),
            dma((CHUNKS,)),
            dma((CHUNKS + 1,)),
            dma((n_ctx,)),
            dma((n_ctx,)),
            dma(()),
            dma((4,)),
        ],
        compiler_params=pltpu.CompilerParams(
            collective_id=0, has_side_effects=True, vmem_limit_bytes=60 * 2**20
        ),
        cost_estimate=pl.CostEstimate(
            flops=4 * tok * heads * tok * SPAN * hd,
            bytes_accessed=4 * tok * heads * hd,
            transcendentals=tok * heads * tok * SPAN,
        ),
    )(queries, kv_cols, lengths, page_owner.reshape(1, -1))
    return attended, cache.reshape(n_ctx * CAP, PAGE, hd)


def solution(mesh):
    in_specs = (P("ctx", "grp"), P("ctx", "grp"), P(), P("ctx", None))
    out_specs = (P("ctx", "grp"), P("ctx", None, "grp"))
    return jax.shard_map(
        functools.partial(per_device, mesh.shape["ctx"]),
        mesh=mesh, in_specs=in_specs, out_specs=out_specs, check_vma=False,
    )
```

time: 42.4 us -> 32.6 us (0.77)
  the two profiles are of different devices: /device:TPU:1 before, /device:TPU:6 now
where the time goes in v2:
time: 32.6 us; the launch traced here: 32.5 us
  Pallas kernels  30.3 us (93%)
  local copies, waits for them, and re-layouts  1.5 us (5%)
  between operations  0.64 us (2%)
    pallas_call x1, Pallas kernels, per_device(): pl.pallas_call(functools.partial(kernel, n_ctx, lengths.shape[0]), out_sh...  30.3 us
    unnamed x2, local copies, waits for them, and re-layouts  1.5 us

profile of v2, /device:TPU:6, one launch (start us, length us, event | category | flops | bytes accessed | tf_op | source)
XLA Modules:
  0.0 32.5 jit_solution(16624255095268184390)
XLA Ops:
  0.6 30.3 %shard_map.59 = (bf16[512,512]{1,0:T(8,128)(2,1)S(1)}, bf16[1024,128]{1,0:T(8,128)(2,1)S(1)}) custom-call(bf16[512,512]{1,0:T(8,128)(2,1)} %q_hbm.1, bf16[512,128]{1,0:T(8,128)(2,1)} %kv_hbm.1, s32[16]{0:T(128)} %len_hbm.1, s32[1,32]{1,0:T(1,128)} %bitcast.3), custom_call_target="tpu_custom_call" | custom-call | flops 2147483648 | bytes 1048576 | tf_op jit(solution)/shard_map/pallas_call | solution.py:308
  31.0 0.8 %copy.8 = bf16[512,512]{1,0:T(8,128)(2,1)} copy(bf16[512,512]{1,0:T(8,128)(2,1)S(1)} %get-tuple-element.6) | data formatting | bytes 1048576
  31.8 0.7 %copy.9 = bf16[64,16,128]{2,1,0:T(8,128)(2,1)} copy(bf16[64,16,128]{2,1,0:T(8,128)(2,1)S(1)} %bitcast.2) | data formatting | bytes 524288

commit v3 on v2

--- a/solution.py
+++ b/solution.py
@@ -13,7 +13,9 @@
 CAP = 2
 Y = 4
 CHUNKS = 4
-WINDOW = 4
+ANSWER_AT = 1
+ANSWER_ROWS = 8
+RELAYED = 3
 BIG = float(2**20)
 MESH = pl.DeviceIdType.MESH
 
@@ -104,8 +106,9 @@
             device_id=(c + d, g), device_id_type=MESH,
         )
 
-    def is_ahead(d):
+    def is_ahead(d, i):
         far_off = (a == 0) if d == 3 else (a == Y - 1) if d == 1 else False
+        far_off = far_off if i < RELAYED else False
         return (c + d < n_ctx) & jnp.logical_not(far_off)
 
     def onward(i):
@@ -142,17 +145,13 @@
     def receive(i):
         for d in (2, 1, 3, 4):
             pl.when(c >= d)(came(d, i).wait_recv)
-            if d == 2:
+            if d == 2 and i < RELAYED:
                 pl.when(goes_on)(onward(i).start)
         far_to_partner(kind, i).start()
 
     def send(i):
         for d in (2, 1, 3, 4):
-            pl.when(is_ahead(d))(ahead(d, i).start)
-
-    for i in range(WINDOW):
-        send(i)
-    own_to_partner(kind).start()
+            pl.when(is_ahead(d, i))(ahead(d, i).start)
 
     def slots_of(p):
         return pl.ds(p * rows_per_owner, rows_per_owner)
@@ -160,30 +159,43 @@
     def page_to(p):
         return pltpu.make_async_remote_copy(
             src_ref=outgoing.at[slots_of(p), :], dst_ref=cache_ref.at[slots_of(c), :],
-            send_sem=send_page.at[p], recv_sem=recv_page.at[c],
+            send_sem=send_page, recv_sem=recv_page.at[z],
             device_id=(p, g), device_id_type=MESH,
         )
 
-    def page_from(p):
-        return pltpu.make_async_remote_copy(
-            src_ref=outgoing.at[slots_of(p), :], dst_ref=cache_ref.at[slots_of(p), :],
-            send_sem=send_page.at[p], recv_sem=recv_page.at[p],
-            device_id=(p, g), device_id_type=MESH,
-        )
-
-    def others(first, last, act):
+    def pages_from(row_z, count):
+        return pltpu.make_async_remote_copy(
+            src_ref=outgoing.at[pl.ds(0, count * rows_per_owner), :],
+            dst_ref=cache_ref.at[pl.ds(row_z * Y * rows_per_owner, count * rows_per_owner), :],
+            send_sem=send_page, recv_sem=recv_page.at[row_z],
+            device_id=(c, partner), device_id_type=MESH,
+        )
+
+    def send_pages(first, last):
         def body(p, carry):
-            pl.when(p != c)(functools.partial(act, p))
+            pl.when(p != c)(page_to(p).start)
             return carry
 
         lax.fori_loop(first, last, body, 0)
+
+    def answer(first_z, last_z):
+        def body(row_z, carry):
+            pages_from(row_z, Y).wait_recv()
+            for k in range(Y):
+                page_to(row_z * Y + k).start()
+            return carry
+
+        lax.fori_loop(first_z, last_z, body, 0)
 
     own_pages = pltpu.make_async_copy(
         outgoing.at[slots_of(c), :], cache_ref.at[slots_of(c), :], own_page
     )
     own_pages.start()
 
-    others(0, row0 + Y, lambda p: page_to(p).start())
+    send_pages(0, row0 + Y)
+    own_to_partner(kind).start()
+    send(0)
+    send(1)
 
     load_len.wait()
     lane = lax.broadcasted_iota(jnp.int32, (1, hd), 1)
@@ -267,34 +279,54 @@
             tags = kaug[i, : near * chunk]
             unit(keys, values, tags, head, r0, half, 0, False, False, i == CHUNKS - 1)
 
+    last_z = jnp.minimum(z + 1 + ANSWER_ROWS, top_z + 1)
     own_to_partner(1 - kind).wait_recv()
     for head in range(heads):
         diagonal(head)
     receive(0)
+    send(2)
+    send(3)
     for i in range(CHUNKS):
         far_to_partner(1 - kind, i).wait_recv()
         for head in range(heads):
             if head == heads // 2 and i + 1 < CHUNKS:
-                if i + WINDOW < CHUNKS:
-                    send(i + WINDOW)
                 receive(i + 1)
             earlier(i, head)
-
-    def answer(p):
-        page_from(p).wait_recv()
-        page_to(p).start()
-
-    others(row0 + Y, n_ctx, answer)
+        if i == ANSWER_AT:
+            answer(z + 1, last_z)
+
+    answer(last_z, top_z + 1)
 
     own_to_partner(kind).wait_send()
     for i in range(CHUNKS):
         far_to_partner(kind, i).wait_send()
         for d in range(1, SPAN + 1):
-            pl.when(is_ahead(d))(ahead(d, i).wait_send)
-        pl.when(goes_on)(onward(i).wait_send)
-    others(0, row0 + Y, lambda p: page_from(p).wait_recv())
-    others(0, n_ctx, lambda p: page_to(p).wait_send())
+            pl.when(is_ahead(d, i))(ahead(d, i).wait_send)
+        if i < RELAYED:
+            pl.when(goes_on)(onward(i).wait_send)
+    def pages_in(row_z, carry):
+        pages_from(row_z, Y).wait_recv()
+        return carry
+
+    lax.fori_loop(0, z, pages_in, 0)
+    pages_from(z, Y - 1).wait_recv()
+    sent = outgoing.at[pl.ds(0, (n_ctx - 1) * rows_per_owner), :]
+    pltpu.make_async_remote_copy(
+        src_ref=sent, dst_ref=sent, send_sem=send_page, recv_sem=recv_page.at[z],
+        device_id=(c, partner), device_id_type=MESH,
+    ).wait_send()
     own_pages.wait()
+
+
+def place(att_ref, cache_ref, att_out, cache_out, done):
+    copies = [
+        pltpu.make_async_copy(att_ref, att_out, done.at[0]),
+        pltpu.make_async_copy(cache_ref, cache_out, done.at[1]),
+    ]
+    for copy in copies:
+        copy.start()
+    for copy in copies:
+        copy.wait()
 
 
 def per_device(n_ctx, queries, kv_cols, lengths, page_owner):
@@ -326,8 +358,8 @@
             dma((SPAN + 1, CHUNKS)),
             dma((CHUNKS,)),
             dma((CHUNKS + 1,)),
-            dma((n_ctx,)),
-            dma((n_ctx,)),
+            dma((n_ctx // Y,)),
+            dma(()),
             dma(()),
             dma((4,)),
         ],
@@ -340,6 +372,17 @@
             transcendentals=tok * heads * tok * SPAN,
         ),
     )(queries, kv_cols, lengths, page_owner.reshape(1, -1))
+    attended, cache = pl.pallas_call(
+        place,
+        out_shape=(
+            jax.ShapeDtypeStruct(queries.shape, bf16),
+            jax.ShapeDtypeStruct((slots, hd), bf16),
+        ),
+        in_specs=[vmem, vmem],
+        out_specs=(hbm, hbm),
+        scratch_shapes=[dma((2,))],
+        compiler_params=pltpu.CompilerParams(vmem_limit_bytes=2**20),
+    )(attended, cache)
     return attended, cache.reshape(n_ctx * CAP, PAGE, hd)
 
 

time: 32.6 us -> 29.1 us (0.89)
  the two profiles are of different devices: /device:TPU:6 before, /device:TPU:449 now
where the time goes in v3:
time: 29.1 us; the launch traced here: 29 us
  Pallas kernels  28.4 us (98%)
  between operations  0.64 us (2%)
    pallas_call x1, Pallas kernels, per_device(): pl.pallas_call(functools.partial(kernel, n_ctx, lengths.shape[0]), out_sh...  27.5 us
    pallas_call x1, Pallas kernels, per_device(): pl.pallas_call(place, out_shape=(jax.ShapeDtypeStruct(queries.shape, bf16...  0.89 us

profile of v3, /device:TPU:449, one launch (start us, length us, event | category | flops | bytes accessed | tf_op | source)
XLA Modules:
  0.0 29.0 jit_solution(2513659103174631040)
XLA Ops:
  0.6 27.5 %shard_map.59 = (bf16[512,512]{1,0:T(8,128)(2,1)S(1)}, bf16[1024,128]{1,0:T(8,128)(2,1)S(1)}) custom-call(bf16[512,512]{1,0:T(8,128)(2,1)} %q_hbm.1, bf16[512,128]{1,0:T(8,128)(2,1)} %kv_hbm.1, s32[16]{0:T(128)} %len_hbm.1, s32[1,32]{1,0:T(1,128)} %bitcast.3), custom_call_target="tpu_custom_call" | custom-call | flops 2147483648 | bytes 1048576 | tf_op jit(solution)/shard_map/pallas_call | solution.py:340
  28.1 0.9 %shard_map.60 = (bf16[512,512]{1,0:T(8,128)(2,1)}, bf16[1024,128]{1,0:T(8,128)(2,1)}) custom-call(bf16[512,512]{1,0:T(8,128)(2,1)S(1)} %get-tuple-element.6.att_ref, bf16[1024,128]{1,0:T(8,128)(2,1)S(1)} %get-tuple-element.7.cache_ref), custom_call_target="tpu_custom_call" | custom-call | tf_op jit(solution)/shard_map/pallas_call | solution.py:375

commit v4 on v3

--- a/solution.py
+++ b/solution.py
@@ -15,7 +15,7 @@
 CHUNKS = 4
 ANSWER_AT = 1
 ANSWER_ROWS = 8
-RELAYED = 3
+RELAYED = 1
 BIG = float(2**20)
 MESH = pl.DeviceIdType.MESH
 

time: 29.1 us -> 28.3 us (0.973)
  the two profiles are of different devices: /device:TPU:449 before, /device:TPU:65 now
where the time goes in v4:
time: 28.3 us; the launch traced here: 28.1 us
  Pallas kernels  27.5 us (97%)
  between operations  0.64 us (2%)
    pallas_call x1, Pallas kernels, per_device(): pl.pallas_call(functools.partial(kernel, n_ctx, lengths.shape[0]), out_sh...  26.6 us
    pallas_call x1, Pallas kernels, per_device(): pl.pallas_call(place, out_shape=(jax.ShapeDtypeStruct(queries.shape, bf16...  0.89 us

profile of v4, /device:TPU:65, one launch (start us, length us, event | category | flops | bytes accessed | tf_op | source)
XLA Modules:
  0.0 28.1 jit_solution(13685939604674590205)
XLA Ops:
  0.6 26.6 %shard_map.59 = (bf16[512,512]{1,0:T(8,128)(2,1)S(1)}, bf16[1024,128]{1,0:T(8,128)(2,1)S(1)}) custom-call(bf16[512,512]{1,0:T(8,128)(2,1)} %q_hbm.1, bf16[512,128]{1,0:T(8,128)(2,1)} %kv_hbm.1, s32[16]{0:T(128)} %len_hbm.1, s32[1,32]{1,0:T(1,128)} %bitcast.3), custom_call_target="tpu_custom_call" | custom-call | flops 2147483648 | bytes 1048576 | tf_op jit(solution)/shard_map/pallas_call | solution.py:340
  27.2 0.9 %shard_map.60 = (bf16[512,512]{1,0:T(8,128)(2,1)}, bf16[1024,128]{1,0:T(8,128)(2,1)}) custom-call(bf16[512,512]{1,0:T(8,128)(2,1)S(1)} %get-tuple-element.6.att_ref, bf16[1024,128]{1,0:T(8,128)(2,1)S(1)} %get-tuple-element.7.cache_ref), custom_call_target="tpu_custom_call" | custom-call | tf_op jit(solution)/shard_map/pallas_call | solution.py:375

commit v5 on v4

--- a/solution.py
+++ b/solution.py
@@ -192,8 +192,8 @@
     )
     own_pages.start()
 
+    own_to_partner(kind).start()
     send_pages(0, row0 + Y)
-    own_to_partner(kind).start()
     send(0)
     send(1)
 
@@ -289,7 +289,7 @@
     for i in range(CHUNKS):
         far_to_partner(1 - kind, i).wait_recv()
         for head in range(heads):
-            if head == heads // 2 and i + 1 < CHUNKS:
+            if head == 1 and i + 1 < CHUNKS:
                 receive(i + 1)
             earlier(i, head)
         if i == ANSWER_AT:

time: 28.3 us -> 28.5 us (level)
  Pallas kernels: 27.5 us -> 27.8 us
where the time goes in v5:
time: 28.5 us; the launch traced here: 28.4 us
  Pallas kernels  27.8 us (98%)
  between operations  0.64 us (2%)
    pallas_call x1, Pallas kernels, per_device(): pl.pallas_call(functools.partial(kernel, n_ctx, lengths.shape[0]), out_sh...  26.9 us
    pallas_call x1, Pallas kernels, per_device(): pl.pallas_call(place, out_shape=(jax.ShapeDtypeStruct(queries.shape, bf16...  0.89 us

profile of v5, /device:TPU:65, one launch (start us, length us, event | category | flops | bytes accessed | tf_op | source)
XLA Modules:
  0.0 28.4 jit_solution(13774047199797432227)
XLA Ops:
  0.6 26.9 %shard_map.59 = (bf16[512,512]{1,0:T(8,128)(2,1)S(1)}, bf16[1024,128]{1,0:T(8,128)(2,1)S(1)}) custom-call(bf16[512,512]{1,0:T(8,128)(2,1)} %q_hbm.1, bf16[512,128]{1,0:T(8,128)(2,1)} %kv_hbm.1, s32[16]{0:T(128)} %len_hbm.1, s32[1,32]{1,0:T(1,128)} %bitcast.3), custom_call_target="tpu_custom_call" | custom-call | flops 2147483648 | bytes 1048576 | tf_op jit(solution)/shard_map/pallas_call | solution.py:340
  27.5 0.9 %shard_map.60 = (bf16[512,512]{1,0:T(8,128)(2,1)}, bf16[1024,128]{1,0:T(8,128)(2,1)}) custom-call(bf16[512,512]{1,0:T(8,128)(2,1)S(1)} %get-tuple-element.6.att_ref, bf16[1024,128]{1,0:T(8,128)(2,1)S(1)} %get-tuple-element.7.cache_ref), custom_call_target="tpu_custom_call" | custom-call | tf_op jit(solution)/shard_map/pallas_call | solution.py:375
